TPU v7x, 32 devices: a whole 2x2x4 slice. The times are simulated.
32 devices in a mesh: rep: 2 (over x), gx: 16 (over z, y, core).
Axes of the slice: x: 2, y: 2, z: 4, core: 2. Of those that a mesh axis runs over, the one named last changes fastest.
Arguments:
- in_field: bfloat16 [64, 16, 64, 128], P(('rep', 'gx')), parts along dimension 0, may hold values from -6 to 6
- cotangent: bfloat16 [64, 16, 64, 128], P(('rep', 'gx')), parts along dimension 0, may hold values from -6 to 6
- spec_weight: bfloat16 [256, 64, 128], P('gx'), may hold values from -4 to 4
- w_in: bfloat16 [64, 128], replicated, may hold values from -0.75 to 0.75
- w_out: bfloat16 [128, 64], replicated, may hold values from -0.5 to 0.5
Outputs:
- grad_field: bfloat16 [64, 16, 64, 128], P(('rep', 'gx')), parts along dimension 0
- grad_spec: float32 [512, 64, 128], P(('rep', 'gx')), parts along dimension 0
- grad_w_in: float32 [128, 128], P('rep'), parts along dimension 0
- grad_w_out: float32 [256, 64], P('rep'), parts along dimension 0
There are 2 independent parts, one for each index of `rep`. A program takes and returns all parts, laid end to end along the dimension named above; an argument that names none is the same for every part. Nothing has to cross between parts.
All inputs are finite; a program needn't handle non-finite values.
Results may differ from a plain program's by a relative error of at most 0.01.
Values may be sent and summed in bfloat16 or wider, within the bound.
A program may use at most 128 MiB of HBM per device.

v0:
```python
import math

import jax
import jax.numpy as jnp
from jax import lax
from jax.sharding import PartitionSpec as P

KZ = 16
KX = 16


def make_tables(length_x, length_z):
    z_pos = jnp.arange(length_z, dtype=jnp.int32)
    k_z = jnp.arange(KZ, dtype=jnp.int32)
    angle_z = (
        2.0 * math.pi * (k_z[:, None] * z_pos[None, :] % length_z).astype(jnp.float32) / length_z
    )
    cos_z = jnp.cos(angle_z)
    sin_z = jnp.sin(angle_z)
    k_weight = jnp.where(k_z == 0, 1.0, 2.0).astype(jnp.float32)[:, None]
    forward_z = (jnp.concatenate([cos_z, -sin_z], 0).T / math.sqrt(length_z)).astype(jnp.bfloat16)
    inverse_z = (
        jnp.concatenate([k_weight * cos_z, -k_weight * sin_z], 0) / math.sqrt(length_z)
    ).astype(jnp.bfloat16)
    j_index = jnp.arange(KX, dtype=jnp.int32)
    k_x = jnp.where(j_index < KX // 2, j_index, length_x - KX + j_index)
    x_pos = jnp.arange(length_x, dtype=jnp.int32)
    angle_x = (
        2.0 * math.pi * (k_x[:, None] * x_pos[None, :] % length_x).astype(jnp.float32) / length_x
    )
    cosine_x = jnp.cos(angle_x) / math.sqrt(length_x)
    sine_x = jnp.sin(angle_x) / math.sqrt(length_x)
    return (forward_z, inverse_z, cosine_x, sine_x)


def x_halves(pencil, cos_b, sin_b):
    f32 = jnp.float32
    real_part = pencil[..., :KZ]
    imag_part = pencil[..., KZ:]
    out_real = jnp.einsum(
        "jx,xyck->yjkc", cos_b, real_part, preferred_element_type=f32
    ) + jnp.einsum("jx,xyck->yjkc", sin_b, imag_part, preferred_element_type=f32)
    out_imag = jnp.einsum(
        "jx,xyck->yjkc", cos_b, imag_part, preferred_element_type=f32
    ) - jnp.einsum("jx,xyck->yjkc", sin_b, real_part, preferred_element_type=f32)
    return (out_real, out_imag)


def join_halves(halves):
    joined = jnp.concatenate([halves[0], halves[1]], -1)
    return joined.reshape(joined.shape[0], KX * KZ, joined.shape[-1])


def x_inverse(spectrum, cosine_x, sine_x):
    rows = spectrum.shape[0]
    chans = spectrum.shape[-1] // 2
    shaped = spectrum.reshape(rows, KX, KZ, 2 * chans)
    real_part = shaped[..., :chans]
    imag_part = shaped[..., chans:]
    high = lax.Precision.HIGHEST
    out_real = jnp.einsum("jx,yjkc->xyck", cosine_x, real_part, precision=high) - jnp.einsum(
        "jx,yjkc->xyck", sine_x, imag_part, precision=high
    )
    out_imag = jnp.einsum("jx,yjkc->xyck", cosine_x, imag_part, precision=high) + jnp.einsum(
        "jx,yjkc->xyck", sine_x, real_part, precision=high
    )
    return jnp.concatenate([out_real, out_imag], -1)


def mixing(spectrum, weight):
    chans = weight.shape[1]
    high = lax.Precision.HIGHEST
    prod_real = jnp.einsum("ymc,mcf->ymf", spectrum[..., :chans], weight, precision=high)
    prod_imag = jnp.einsum("ymc,mcf->ymf", spectrum[..., chans:], weight, precision=high)
    return jnp.concatenate(
        [
            prod_real[..., :chans] - prod_imag[..., chans:],
            prod_real[..., chans:] + prod_imag[..., :chans],
        ],
        -1,
    )


def mixing_back(d_spectrum, spectrum, weight):
    chans = weight.shape[1]
    high = lax.Precision.HIGHEST
    d_real = d_spectrum[..., :chans]
    d_imag = d_spectrum[..., chans:]
    d_cat = jnp.concatenate([d_real, d_imag], -1)
    d_rot = jnp.concatenate([d_imag, -d_real], -1)
    d_xr = jnp.einsum("ymf,mcf->ymc", d_cat, weight, precision=high)
    d_xi = jnp.einsum("ymf,mcf->ymc", d_rot, weight, precision=high)
    grads = jnp.einsum("ymc,ymf->mcf", spectrum[..., :chans], d_cat, precision=high)
    grads = grads + jnp.einsum("ymc,ymf->mcf", spectrum[..., chans:], d_rot, precision=high)
    return (jnp.concatenate([d_xr, d_xi], -1), grads)


def pointwise(in_slab, cot_slab, inverse_b, w_in, w_out, inverse_z):
    f32 = jnp.float32
    spectral = jnp.einsum("xyck,kz->xycz", inverse_b, inverse_z, preferred_element_type=f32)
    hidden = jnp.einsum("xycz,ch->xyhz", in_slab, w_in, preferred_element_type=f32)
    act_b = jax.nn.gelu(hidden).astype(jnp.bfloat16)
    branch = jnp.einsum("xyhz,hc->xycz", act_b, w_out, preferred_element_type=f32)
    pre = spectral + branch
    unused_t, pull_t = jax.vjp(jax.nn.gelu, pre)
    d_pre = pull_t(cot_slab.astype(f32))[0].astype(jnp.bfloat16)
    d_hidden = jnp.einsum("xycz,hc->xyhz", d_pre, w_out, preferred_element_type=f32)
    unused_h, pull_h = jax.vjp(jax.nn.gelu, hidden)
    d_act = pull_h(d_hidden)[0].astype(jnp.bfloat16)
    du_mlp = jnp.einsum("xyhz,ch->xycz", d_act, w_in, preferred_element_type=f32)
    dw_out = jnp.einsum("xyhz,xycz->hc", act_b, d_pre, preferred_element_type=f32)
    dw_in = jnp.einsum("xycz,xyhz->ch", in_slab, d_act, preferred_element_type=f32)
    d_inverse = jnp.einsum("xycz,kz->xyck", d_pre, inverse_z, preferred_element_type=f32).astype(
        jnp.bfloat16
    )
    return (d_inverse, du_mlp, dw_in, dw_out)


def body(in_field, cotangent, spec_weight, w_in, w_out):
    f32 = jnp.float32
    devices_x = lax.axis_size("gx")
    planes = in_field.shape[0]
    rows_all = in_field.shape[1]
    z_cells = in_field.shape[3]
    length_x = planes * devices_x
    forward_z, inverse_z, cosine_x, sine_x = make_tables(length_x, z_cells)
    cos_b = cosine_x.astype(jnp.bfloat16)
    sin_b = sine_x.astype(jnp.bfloat16)

    def transform_x(pencil):
        return x_halves(pencil, cos_b, sin_b)

    coeffs = jnp.einsum("xycz,zk->xyck", in_field, forward_z, preferred_element_type=f32).astype(
        jnp.bfloat16
    )
    pencil = lax.all_to_all(coeffs, "gx", split_axis=1, concat_axis=0, tiled=True)
    spectrum = join_halves(transform_x(pencil))
    owned_spec = lax.all_to_all(spectrum, "gx", split_axis=1, concat_axis=0, tiled=True)
    weight_f = spec_weight.astype(f32)
    returned = lax.all_to_all(
        mixing(owned_spec, weight_f), "gx", split_axis=0, concat_axis=1, tiled=True
    )
    inverse_b = x_inverse(returned, cosine_x, sine_x).astype(jnp.bfloat16)
    back_slabs = lax.all_to_all(inverse_b, "gx", split_axis=0, concat_axis=1, tiled=True)
    d_inverse, du_mlp, dw_in, dw_out = pointwise(
        in_field, cotangent, back_slabs, w_in, w_out, inverse_z
    )
    dw_in, dw_out = lax.psum((dw_in, dw_out), "gx")
    grad_pencil = lax.all_to_all(d_inverse, "gx", split_axis=1, concat_axis=0, tiled=True)
    d_mixed = join_halves(transform_x(grad_pencil))
    d_owned = lax.all_to_all(d_mixed, "gx", split_axis=1, concat_axis=0, tiled=True)
    d_local, grad_spec = mixing_back(d_owned, owned_spec, weight_f)
    d_returned = lax.all_to_all(d_local, "gx", split_axis=0, concat_axis=1, tiled=True)
    d_coeffs = x_inverse(d_returned, cosine_x, sine_x).astype(jnp.bfloat16)
    grad_slabs = lax.all_to_all(d_coeffs, "gx", split_axis=0, concat_axis=1, tiled=True)
    du_spec = jnp.einsum("xyck,zk->xycz", grad_slabs, forward_z, preferred_element_type=f32)
    grad_field = (du_spec + du_mlp).astype(jnp.bfloat16)
    grad_scale = 1.0 / math.sqrt(length_x * rows_all * z_cells)
    return (grad_field, grad_spec, dw_in * grad_scale, dw_out * grad_scale)


def solution(mesh):
    placed = (
        P(("rep", "gx"), None, None, None),
        P(("rep", "gx"), None, None, None),
        P("gx", None, None),
        P(),
        P(),
    )
    return jax.shard_map(
        body,
        mesh=mesh,
        in_specs=placed,
        out_specs=(
            P(("rep", "gx"), None, None, None),
            P(("rep", "gx"), None, None),
            P("rep", None),
            P("rep", None),
        ),
        check_vma=False,
    )
```

profile of v0, /device:TPU:0, one launch (start us, length us, event | category | flops | bytes accessed | tf_op | source)
XLA Modules:
  0.0 209.5 jit_solution(2553081415425587274)
XLA Ops:
  9.8 7.4 %all-to-all-start = ((bf16[16,2,2048]{2,1,0:T(2,128)(2,1)}), bf16[16,2,2048]{2,1,0:T(2,128)(2,1)S(1)}, u32[]{:S(2)}, u32[]{:S(2)}) async-start(bf16[16,2,2048]{2,1,0:T(2,128)(2,1)} %reshape.189), calls=%async_computation | async-start | bytes 262144 | tf_op jit(solution)/shard_map/all_to_all | solution.py:136
  17.2 7.9 %all-to-all-done = bf16[16,2,2048]{2,1,0:T(2,128)(2,1)S(1)} async-done(((bf16[16,2,2048]{2,1,0:T(2,128)(2,1)}), bf16[16,2,2048]{2,1,0:T(2,128)(2,1)S(1)}, u32[]{:S(2)}, u32[]{:S(2)}) %all-to-all-start) | async-done | bytes 131104 | tf_op jit(solution)/shard_map/all_to_all | solution.py:136
  27.2 3.5 %all-to-all-start.1 = ((f32[1,256,128]{2,0,1:T(1,128)}), f32[1,256,128]{2,0,1:T(1,128)S(1)}, u32[]{:S(2)}, u32[]{:S(2)}) async-start(f32[1,256,128]{2,0,1:T(1,128)} %bitcast.17), calls=%async_computation.1 | async-start | bytes 262144 | tf_op jit(solution)/shard_map/all_to_all | solution.py:138
  30.7 7.9 %all-to-all-done.1 = f32[1,256,128]{2,0,1:T(1,128)S(1)} async-done(((f32[1,256,128]{2,0,1:T(1,128)}), f32[1,256,128]{2,0,1:T(1,128)S(1)}, u32[]{:S(2)}, u32[]{:S(2)}) %all-to-all-start.1) | async-done | bytes 131104 | tf_op jit(solution)/shard_map/all_to_all | solution.py:138
  40.3 3.5 %all-to-all-start.2 = ((f32[16,16,128]{2,1,0:T(8,128)}), f32[16,16,128]{2,1,0:T(8,128)S(1)}, u32[]{:S(2)}, u32[]{:S(2)}) async-start(f32[16,16,128]{2,1,0:T(8,128)} %copy.59), calls=%async_computation.2 | async-start | bytes 262144 | tf_op jit(solution)/shard_map/all_to_all | solution.py:140
  43.9 1.8 fusion.59
  45.7 6.1 %all-to-all-done.2 = f32[16,16,128]{2,1,0:T(8,128)S(1)} async-done(((f32[16,16,128]{2,1,0:T(8,128)}), f32[16,16,128]{2,1,0:T(8,128)S(1)}, u32[]{:S(2)}, u32[]{:S(2)}) %all-to-all-start.2) | async-done | bytes 131104 | tf_op jit(solution)/shard_map/all_to_all | solution.py:140
  55.1 3.5 %all-to-all-start.3 = ((bf16[16,2,2048]{2,1,0:T(2,128)(2,1)}), bf16[16,2,2048]{2,1,0:T(2,128)(2,1)S(1)}, u32[]{:S(2)}, u32[]{:S(2)}) async-start(bf16[16,2,2048]{2,1,0:T(2,128)(2,1)} %reshape.191), calls=%async_computation.3 | async-start | bytes 262144 | tf_op jit(solution)/shard_map/all_to_all | solution.py:144
  58.7 7.8 %all-to-all-done.3 = bf16[16,2,2048]{2,1,0:T(2,128)(2,1)S(1)} async-done(((bf16[16,2,2048]{2,1,0:T(2,128)(2,1)}), bf16[16,2,2048]{2,1,0:T(2,128)(2,1)S(1)}, u32[]{:S(2)}, u32[]{:S(2)}) %all-to-all-start.3) | async-done | bytes 131104 | tf_op jit(solution)/shard_map/all_to_all | solution.py:144
  67.1 3.3 %fusion.29 = bf16[2,16,64,128]{3,2,1,0:T(8,128)(2,1)S(1)} fusion(bf16[2,16,64,128]{3,2,1,0:T(8,128)(2,1)S(1)} %copy-done.8, f32[2,16,64,128]{3,2,1,0:T(8,128)S(1)} %fusion.39, bf16[128,64]{0,1:T(8,128)(2,1)S(1)} %copy-done.9, f32[128,2,16,128]{3,0,2,1:T(8,128)} %fusion.59), kind=kOutput, calls=%fused_computation.57 | convolution fusion | flops 77594624 | bytes 4210688 | tf_op jit(solution)/shard_map/xyhz,hc->xycz/dot_general | solution.py:103
  70.4 1.7 fusion.6
  73.6 3.5 %all-to-all-start.4 = ((bf16[16,2,2048]{2,1,0:T(2,128)(2,1)}), bf16[16,2,2048]{2,1,0:T(2,128)(2,1)S(1)}, u32[]{:S(2)}, u32[]{:S(2)}) async-start(bf16[16,2,2048]{2,1,0:T(2,128)(2,1)} %reshape.193), calls=%async_computation.4 | async-start | bytes 262144 | tf_op jit(solution)/shard_map/all_to_all | solution.py:149
  77.2 3.1 %convolution_bitcast_fusion.6 = f32[128,64]{0,1:T(8,128)} fusion(bf16[2,16,64,128]{3,2,1,0:T(8,128)(2,1)S(1)} %fusion.29, f32[128,2,16,128]{3,0,2,1:T(8,128)} %fusion.59), kind=kOutput, calls=%fused_computation.53 | convolution fusion | flops 71827456 | bytes 2654208 | tf_op jit(solution)/shard_map/xyhz,xycz->hc/dot_general | solution.py:111
  80.2 1.1 convolution_bitcast_fusion.7
  81.4 3.6 %all-to-all-done.4 = bf16[16,2,2048]{2,1,0:T(2,128)(2,1)S(1)} async-done(((bf16[16,2,2048]{2,1,0:T(2,128)(2,1)}), bf16[16,2,2048]{2,1,0:T(2,128)(2,1)S(1)}, u32[]{:S(2)}, u32[]{:S(2)}) %all-to-all-start.4) | async-done | bytes 131104 | tf_op jit(solution)/shard_map/all_to_all | solution.py:149
  87.1 3.7 %all-to-all-start.5 = ((f32[1,256,128]{2,0,1:T(1,128)}), f32[1,256,128]{2,0,1:T(1,128)S(1)}, u32[]{:S(2)}, u32[]{:S(2)}) async-start(f32[1,256,128]{2,0,1:T(1,128)} %bitcast.53), calls=%async_computation.5 | async-start | bytes 262144 | tf_op jit(solution)/shard_map/all_to_all | solution.py:151
  90.8 77.6 %all-reduce.3.cloned.1.call-done = (f32[64,128]{1,0:T(8,128)}, f32[128,64]{0,1:T(8,128)}) async-done(((f32[64,128]{1,0:T(8,128)}, f32[128,64]{0,1:T(8,128)}), (f32[64,128]{1,0:T(8,128)}, f32[128,64]{0,1:T(8,128)})) %all-reduce.3.cloned.1.call-update) | async-done | bytes 65552 | tf_op jit(solution)/shard_map/psum | solution.py:148
  168.4 1.4 broadcast_multiply_fusion.1
  171.9 6.4 %all-to-all-start.6 = ((f32[16,16,128]{2,1,0:T(8,128)}), f32[16,16,128]{2,1,0:T(8,128)S(1)}, u32[]{:S(2)}, u32[]{:S(2)}) async-start(f32[16,16,128]{2,1,0:T(8,128)} %copy.71), calls=%async_computation.6 | async-start | bytes 262144 | tf_op jit(solution)/shard_map/all_to_all | solution.py:153
  179.9 6.3 %all-to-all-done.6 = f32[16,16,128]{2,1,0:T(8,128)S(1)} async-done(((f32[16,16,128]{2,1,0:T(8,128)}), f32[16,16,128]{2,1,0:T(8,128)S(1)}, u32[]{:S(2)}, u32[]{:S(2)}) %all-to-all-start.6) | async-done | bytes 131104 | tf_op jit(solution)/shard_map/all_to_all | solution.py:153
  189.5 3.5 %all-to-all-start.7 = ((bf16[16,2,2048]{2,1,0:T(2,128)(2,1)}), bf16[16,2,2048]{2,1,0:T(2,128)(2,1)S(1)}, u32[]{:S(2)}, u32[]{:S(2)}) async-start(bf16[16,2,2048]{2,1,0:T(2,128)(2,1)} %reshape.195), calls=%async_computation.7 | async-start | bytes 262144 | tf_op jit(solution)/shard_map/all_to_all | solution.py:155
  193.1 1.9 convolution_add_fusion
  194.9 6.0 %all-to-all-done.7 = bf16[16,2,2048]{2,1,0:T(2,128)(2,1)S(1)} async-done(((bf16[16,2,2048]{2,1,0:T(2,128)(2,1)}), bf16[16,2,2048]{2,1,0:T(2,128)(2,1)S(1)}, u32[]{:S(2)}, u32[]{:S(2)}) %all-to-all-start.7) | async-done | bytes 131104 | tf_op jit(solution)/shard_map/all_to_all | solution.py:155
  201.5 1.1 fusion.13
  (84 shorter events, 21.3 us)
Async XLA Ops:
  7.2 1.1 copy-start
  7.2 0.6 copy-start.3
  8.8 29.9 %copy-start.1 = (bf16[16,64,128]{2,1,0:T(8,128)(2,1)S(1)}, bf16[16,64,128]{2,1,0:T(8,128)(2,1)}, u32[]{:S(2)}) copy-start(bf16[16,64,128]{2,1,0:T(8,128)(2,1)} %param.7) | copy-start | bytes 786436
  9.8 15.3 %all-to-all-start = ((bf16[16,2,2048]{2,1,0:T(2,128)(2,1)}), bf16[16,2,2048]{2,1,0:T(2,128)(2,1)S(1)}, u32[]{:S(2)}, u32[]{:S(2)}) async-start(bf16[16,2,2048]{2,1,0:T(2,128)(2,1)} %reshape.189), calls=%async_computation | async-start | bytes 262144 | tf_op jit(solution)/shard_map/all_to_all | solution.py:136
  26.4 17.5 %copy-start.5 = (bf16[64,128]{1,0:T(8,128)(2,1)S(1)}, bf16[64,128]{1,0:T(8,128)(2,1)}, u32[]{:S(2)}) copy-start(bf16[64,128]{1,0:T(8,128)(2,1)} %param.8) | copy-start | bytes 49156
  27.2 11.4 %all-to-all-start.1 = ((f32[1,256,128]{2,0,1:T(1,128)}), f32[1,256,128]{2,0,1:T(1,128)S(1)}, u32[]{:S(2)}, u32[]{:S(2)}) async-start(f32[1,256,128]{2,0,1:T(1,128)} %bitcast.17), calls=%async_computation.1 | async-start | bytes 262144 | tf_op jit(solution)/shard_map/all_to_all | solution.py:138
  40.3 11.4 %all-to-all-start.2 = ((f32[16,16,128]{2,1,0:T(8,128)}), f32[16,16,128]{2,1,0:T(8,128)S(1)}, u32[]{:S(2)}, u32[]{:S(2)}) async-start(f32[16,16,128]{2,1,0:T(8,128)} %copy.59), calls=%async_computation.2 | async-start | bytes 262144 | tf_op jit(solution)/shard_map/all_to_all | solution.py:140
  53.4 13.6 %copy-start.8 = (bf16[2,16,64,128]{3,2,1,0:T(8,128)(2,1)S(1)}, bf16[2,16,64,128]{3,2,1,0:T(8,128)(2,1)}, u32[]{:S(2)}) copy-start(bf16[2,16,64,128]{3,2,1,0:T(8,128)(2,1)} %param.6) | copy-start | bytes 1572868
  53.4 13.6 %copy-start.9 = (bf16[128,64]{0,1:T(8,128)(2,1)S(1)}, bf16[128,64]{0,1:T(8,128)(2,1)}, u32[]{:S(2)}) copy-start(bf16[128,64]{0,1:T(8,128)(2,1)} %param.9) | copy-start | bytes 49156
  55.1 11.4 %all-to-all-start.3 = ((bf16[16,2,2048]{2,1,0:T(2,128)(2,1)}), bf16[16,2,2048]{2,1,0:T(2,128)(2,1)S(1)}, u32[]{:S(2)}, u32[]{:S(2)}) async-start(bf16[16,2,2048]{2,1,0:T(2,128)(2,1)} %reshape.191), calls=%async_computation.3 | async-start | bytes 262144 | tf_op jit(solution)/shard_map/all_to_all | solution.py:144
  67.0 3.3 %copy-start.2 = (f32[128,2,16,128]{3,0,2,1:T(8,128)S(1)}, f32[128,2,16,128]{3,0,2,1:T(8,128)}, u32[]{:S(2)}) copy-start(f32[128,2,16,128]{3,0,2,1:T(8,128)} %fusion.59) | copy-start | bytes 6291460
  73.6 11.4 %all-to-all-start.4 = ((bf16[16,2,2048]{2,1,0:T(2,128)(2,1)}), bf16[16,2,2048]{2,1,0:T(2,128)(2,1)S(1)}, u32[]{:S(2)}, u32[]{:S(2)}) async-start(bf16[16,2,2048]{2,1,0:T(2,128)(2,1)} %reshape.193), calls=%async_computation.4 | async-start | bytes 262144 | tf_op jit(solution)/shard_map/all_to_all | solution.py:149
  77.1 91.3 %all-reduce.3.cloned.1.call-start = ((), (), s32[]{:S(2)}) async-start(), calls=%async_computation.8 | async-start | bytes 131072 | tf_op jit(solution)/shard_map/psum | solution.py:148
  87.1 82.7 %all-to-all-start.5 = ((f32[1,256,128]{2,0,1:T(1,128)}), f32[1,256,128]{2,0,1:T(1,128)S(1)}, u32[]{:S(2)}, u32[]{:S(2)}) async-start(f32[1,256,128]{2,0,1:T(1,128)} %bitcast.53), calls=%async_computation.5 | async-start | bytes 262144 | tf_op jit(solution)/shard_map/all_to_all | solution.py:151
  168.4 9.9 %copy-start.7 = (f32[128,64]{0,1:T(8,128)S(1)}, f32[128,64]{0,1:T(8,128)}, u32[]{:S(2)}) copy-start(f32[128,64]{0,1:T(8,128)} %get-tuple-element.5) | copy-start | bytes 98308
  171.9 14.3 %all-to-all-start.6 = ((f32[16,16,128]{2,1,0:T(8,128)}), f32[16,16,128]{2,1,0:T(8,128)S(1)}, u32[]{:S(2)}, u32[]{:S(2)}) async-start(f32[16,16,128]{2,1,0:T(8,128)} %copy.71), calls=%async_computation.6 | async-start | bytes 262144 | tf_op jit(solution)/shard_map/all_to_all | solution.py:153
  187.9 13.3 %copy-start.4 = (f32[16,128]{1,0:T(8,128)S(1)}, f32[16,128]{1,0:T(8,128)}, u32[]{:S(2)}) copy-start(f32[16,128]{1,0:T(8,128)} %copy-done.3) | copy-start | bytes 24580
  188.5 13.0 %copy-start.6 = (bf16[64,128]{1,0:T(8,128)(2,1)S(1)}, bf16[64,128]{1,0:T(8,128)(2,1)}, u32[]{:S(2)}) copy-start(bf16[64,128]{1,0:T(8,128)(2,1)} %param.8) | copy-start | bytes 49156
  189.5 11.4 %all-to-all-start.7 = ((bf16[16,2,2048]{2,1,0:T(2,128)(2,1)}), bf16[16,2,2048]{2,1,0:T(2,128)(2,1)S(1)}, u32[]{:S(2)}, u32[]{:S(2)}) async-start(bf16[16,2,2048]{2,1,0:T(2,128)(2,1)} %reshape.195), calls=%async_computation.7 | async-start | bytes 262144 | tf_op jit(solution)/shard_map/all_to_all | solution.py:155
Sparse Core Ops, SparseCore 0:
  82.0 86.3 all-reduce.2
where the time goes:
time: 210 us; the launch traced here: 209 us
  waiting for transfers between devices  123 us (59%)
  starting transfers between devices  35.1 us (17%)
  matrix products  24.9 us (12%)
  between operations  14.5 us (7%)
  local copies, waits for them, and re-layouts  8.78 us (4%)
  other arithmetic  2.9 us (1%)
    psum x1, waiting for transfers between devices, body(): dw_in, dw_out = lax.psum((dw_in, dw_out), 'gx')  77.6 us
    all_to_all x1, waiting for transfers between devices, body(): lax.all_to_all(coeffs, 'gx', split_axis=1, concat_axis=0, tiled=True)  7.92 us
    all_to_all x1, waiting for transfers between devices, body(): lax.all_to_all(spectrum, 'gx', split_axis=1, concat_axis=0, tiled=True)  7.89 us
    all_to_all x1, waiting for transfers between devices, body(): lax.all_to_all(inverse_b, 'gx', split_axis=0, concat_axis=1, tiled=True)  7.81 us
    all_to_all x1, starting transfers between devices, body(): lax.all_to_all(coeffs, 'gx', split_axis=1, concat_axis=0, tiled=True)  7.39 us
    all_to_all x1, starting transfers between devices, body(): lax.all_to_all(d_local, 'gx', split_axis=0, concat_axis=1, tiled=True)  6.4 us
    all_to_all x1, waiting for transfers between devices, body(): lax.all_to_all(d_local, 'gx', split_axis=0, concat_axis=1, tiled=True)  6.29 us
    all_to_all x1, waiting for transfers between devices, body(): lax.all_to_all(mixing(owned_spec, weight_f), 'gx', split_axis=0, concat_a...  6.08 us
  transfers between devices with their start and end apart: 9, of which 8 were waited for; matrix products, arithmetic and copies ran while one was open for 6% of the time, Pallas kernels for 0%

commit v1 on v0

--- a/solution.py
+++ b/solution.py
@@ -145,12 +145,43 @@
     d_inverse, du_mlp, dw_in, dw_out = pointwise(
         in_field, cotangent, back_slabs, w_in, w_out, inverse_z
     )
-    dw_in, dw_out = lax.psum((dw_in, dw_out), "gx")
     grad_pencil = lax.all_to_all(d_inverse, "gx", split_axis=1, concat_axis=0, tiled=True)
     d_mixed = join_halves(transform_x(grad_pencil))
-    d_owned = lax.all_to_all(d_mixed, "gx", split_axis=1, concat_axis=0, tiled=True)
+    chans = dw_in.shape[0]
+    lanes = 2 * chans
+    parts = jnp.concatenate([dw_in.reshape(-1, lanes), dw_out.reshape(-1, lanes)], 0)
+    parts = parts.reshape(devices_x, -1, lanes)
+    own_modes = spec_weight.shape[0]
+    rows_own = d_mixed.shape[0]
+    send = jnp.concatenate(
+        [
+            d_mixed.reshape(rows_own, devices_x, own_modes, lanes)
+            .transpose(1, 0, 2, 3)
+            .reshape(devices_x, rows_own * own_modes, lanes),
+            parts,
+        ],
+        1,
+    )
+    got = lax.all_to_all(send, "gx", split_axis=0, concat_axis=0, tiled=True)
+    d_owned = got[:, : rows_own * own_modes].reshape(rows_all, own_modes, lanes)
+    reduced = jnp.sum(got[:, rows_own * own_modes :], 0)
     d_local, grad_spec = mixing_back(d_owned, owned_spec, weight_f)
-    d_returned = lax.all_to_all(d_local, "gx", split_axis=0, concat_axis=1, tiled=True)
+    send = jnp.concatenate(
+        [
+            d_local.reshape(devices_x, rows_own * own_modes, lanes),
+            jnp.broadcast_to(reduced[None], (devices_x,) + reduced.shape),
+        ],
+        1,
+    )
+    got = lax.all_to_all(send, "gx", split_axis=0, concat_axis=0, tiled=True)
+    d_returned = (
+        got[:, : rows_own * own_modes]
+        .reshape(devices_x, rows_own, own_modes, lanes)
+        .transpose(1, 0, 2, 3)
+        .reshape(rows_own, devices_x * own_modes, lanes)
+    )
+    summed = got[:, rows_own * own_modes :].reshape(-1, lanes)
+    dw_in, dw_out = summed[:chans], summed[chans:].reshape(dw_out.shape)
     d_coeffs = x_inverse(d_returned, cosine_x, sine_x).astype(jnp.bfloat16)
     grad_slabs = lax.all_to_all(d_coeffs, "gx", split_axis=0, concat_axis=1, tiled=True)
     du_spec = jnp.einsum("xyck,zk->xycz", grad_slabs, forward_z, preferred_element_type=f32)

time: 210 us -> 126 us (0.60)
  waiting for transfers between devices: 123 us -> 50.4 us
  between operations: 14.5 us -> 1.21 us
  blocking collectives: 0 us -> 11.6 us
  starting transfers between devices: 35.1 us -> 28.5 us
  matrix products: 24.9 us -> 22.2 us
    psum x1 -> x0, waiting for transfers between devices: 77.6 us -> none  [body(): dw_in, dw_out = lax.psum((dw_in, dw_out), 'gx')]
    all_to_all x0 -> x1, blocking collectives: none -> 11.6 us  [body(): got = lax.all_to_all(send, 'gx', split_axis=0, concat_axis=0, tiled=True)]
    all_to_all x2 -> x1, starting transfers between devices: 10.1 us -> 3.52 us  [body(): got = lax.all_to_all(send, 'gx', split_axis=0, concat_axis=0, tiled=True)]
    all_to_all x1, waiting for transfers between devices: 3.65 us -> 7.39 us  [body(): lax.all_to_all(d_inverse, 'gx', split_axis=1, concat_axis=0, tiled=True)]
    dot_general x1, matrix products: 3.08 us -> 0.76 us  [pointwise(): jnp.einsum('xyhz,xycz->hc', act_b, d_pre, preferred_element_type=f32)]
    all_to_all x2 -> x1, waiting for transfers between devices: 6.29 us -> 7.94 us  [body(): got = lax.all_to_all(send, 'gx', split_axis=0, concat_axis=0, tiled=True)]
    unnamed x28 -> x31, local copies, waits for them, and re-layouts: 5.44 us -> 6.23 us
  transfers between devices with their start and end apart: 9 -> 7, of which waited for: 8 -> 7; matrix products, arithmetic and copies ran while one was open for 6% -> 5% of each run, Pallas kernels for 0% -> 0%
where the time goes in v1:
time: 126 us; the launch traced here: 125 us
  waiting for transfers between devices  50.4 us (40%)
  starting transfers between devices  28.5 us (23%)
  matrix products  22.2 us (18%)
  blocking collectives  11.6 us (9%)
  local copies, waits for them, and re-layouts  9.17 us (7%)
  other arithmetic  2.11 us (2%)
    all_to_all x1, blocking collectives, body(): got = lax.all_to_all(send, 'gx', split_axis=0, concat_axis=0, tiled=True)  11.6 us
    all_to_all x1, waiting for transfers between devices, body(): got = lax.all_to_all(send, 'gx', split_axis=0, concat_axis=0, tiled=True)  7.94 us
    all_to_all x1, waiting for transfers between devices, body(): lax.all_to_all(coeffs, 'gx', split_axis=1, concat_axis=0, tiled=True)  7.92 us
    all_to_all x1, waiting for transfers between devices, body(): lax.all_to_all(spectrum, 'gx', split_axis=1, concat_axis=0, tiled=True)  7.89 us
    all_to_all x1, waiting for transfers between devices, body(): lax.all_to_all(mixing(owned_spec, weight_f), 'gx', split_axis=0, concat_a...  7.43 us
    all_to_all x1, waiting for transfers between devices, body(): lax.all_to_all(d_inverse, 'gx', split_axis=1, concat_axis=0, tiled=True)  7.39 us
    all_to_all x1, starting transfers between devices, body(): lax.all_to_all(coeffs, 'gx', split_axis=1, concat_axis=0, tiled=True)  7.39 us
    all_to_all x1, waiting for transfers between devices, body(): lax.all_to_all(inverse_b, 'gx', split_axis=0, concat_axis=1, tiled=True)  7.21 us
  transfers between devices with their start and end apart: 7, of which 7 were waited for; matrix products, arithmetic and copies ran while one was open for 5% of the time, Pallas kernels for 0%

profile of v1, /device:TPU:0, one launch (start us, length us, event | category | flops | bytes accessed | tf_op | source)
XLA Modules:
  0.0 125.2 jit_solution(4918880181933027749)
XLA Ops:
  2.3 0.9 reshape.192
  3.2 7.4 %all-to-all-start = ((bf16[16,2,2048]{2,1,0:T(2,128)(2,1)}), bf16[16,2,2048]{2,1,0:T(2,128)(2,1)S(1)}, u32[]{:S(2)}, u32[]{:S(2)}) async-start(bf16[16,2,2048]{2,1,0:T(2,128)(2,1)} %reshape.192), calls=%async_computation | async-start | bytes 262144 | tf_op jit(solution)/shard_map/all_to_all | solution.py:136
  10.6 7.9 %all-to-all-done = bf16[16,2,2048]{2,1,0:T(2,128)(2,1)S(1)} async-done(((bf16[16,2,2048]{2,1,0:T(2,128)(2,1)}), bf16[16,2,2048]{2,1,0:T(2,128)(2,1)S(1)}, u32[]{:S(2)}, u32[]{:S(2)}) %all-to-all-start) | async-done | bytes 131104 | tf_op jit(solution)/shard_map/all_to_all | solution.py:136
  20.7 3.5 %all-to-all-start.1 = ((f32[1,256,128]{2,0,1:T(1,128)}), f32[1,256,128]{2,0,1:T(1,128)S(1)}, u32[]{:S(2)}, u32[]{:S(2)}) async-start(f32[1,256,128]{2,0,1:T(1,128)} %bitcast.17), calls=%async_computation.1 | async-start | bytes 262144 | tf_op jit(solution)/shard_map/all_to_all | solution.py:138
  24.2 7.9 %all-to-all-done.1 = f32[1,256,128]{2,0,1:T(1,128)S(1)} async-done(((f32[1,256,128]{2,0,1:T(1,128)}), f32[1,256,128]{2,0,1:T(1,128)S(1)}, u32[]{:S(2)}, u32[]{:S(2)}) %all-to-all-start.1) | async-done | bytes 131104 | tf_op jit(solution)/shard_map/all_to_all | solution.py:138
  33.8 3.5 %all-to-all-start.2 = ((f32[16,16,128]{2,1,0:T(8,128)}), f32[16,16,128]{2,1,0:T(8,128)S(1)}, u32[]{:S(2)}, u32[]{:S(2)}) async-start(f32[16,16,128]{2,1,0:T(8,128)} %copy.61), calls=%async_computation.2 | async-start | bytes 262144 | tf_op jit(solution)/shard_map/all_to_all | solution.py:140
  37.8 7.4 %all-to-all-done.2 = f32[16,16,128]{2,1,0:T(8,128)S(1)} async-done(((f32[16,16,128]{2,1,0:T(8,128)}), f32[16,16,128]{2,1,0:T(8,128)S(1)}, u32[]{:S(2)}, u32[]{:S(2)}) %all-to-all-start.2) | async-done | bytes 131104 | tf_op jit(solution)/shard_map/all_to_all | solution.py:140
  47.6 0.9 reshape.194
  48.5 3.5 %all-to-all-start.3 = ((bf16[16,2,2048]{2,1,0:T(2,128)(2,1)}), bf16[16,2,2048]{2,1,0:T(2,128)(2,1)S(1)}, u32[]{:S(2)}, u32[]{:S(2)}) async-start(bf16[16,2,2048]{2,1,0:T(2,128)(2,1)} %reshape.194), calls=%async_computation.3 | async-start | bytes 262144 | tf_op jit(solution)/shard_map/all_to_all | solution.py:144
  52.7 7.2 %all-to-all-done.3 = bf16[16,2,2048]{2,1,0:T(2,128)(2,1)S(1)} async-done(((bf16[16,2,2048]{2,1,0:T(2,128)(2,1)}), bf16[16,2,2048]{2,1,0:T(2,128)(2,1)S(1)}, u32[]{:S(2)}, u32[]{:S(2)}) %all-to-all-start.3) | async-done | bytes 131104 | tf_op jit(solution)/shard_map/all_to_all | solution.py:144
  60.1 1.1 fusion.39
  61.2 2.6 %fusion.29 = bf16[2,16,64,128]{3,2,1,0:T(8,128)(2,1)S(1)} fusion(bf16[2,16,64,128]{3,2,1,0:T(8,128)(2,1)} %param.6, f32[2,16,64,128]{3,2,1,0:T(8,128)S(1)} %fusion.39, bf16[128,64]{0,1:T(8,128)(2,1)} %param.9, f32[128,2,16,128]{3,0,2,1:T(8,128)S(1)} %fusion.62), kind=kOutput, calls=%fused_computation.57 | convolution fusion | flops 77594624 | bytes 4210688 | tf_op jit(solution)/shard_map/xyhz,hc->xycz/dot_general | solution.py:103
  64.6 3.3 %fusion.6 = bf16[2,16,128,128]{3,2,1,0:T(8,128)(2,1)S(1)} fusion(f32[128,2,16,128]{3,0,2,1:T(8,128)} %copy-done.2, bf16[2,16,64,128]{3,2,1,0:T(8,128)(2,1)S(1)} %fusion.29, bf16[128,64]{0,1:T(8,128)(2,1)S(1)} %copy-done.9), kind=kOutput, calls=%fused_computation.8 | convolution fusion | flops 77594624 | bytes 3686400 | tf_op jit(solution)/shard_map/xycz,hc->xyhz/dot_general | solution.py:107
  68.6 0.9 reshape.196
  69.5 3.5 %all-to-all-start.4 = ((bf16[16,2,2048]{2,1,0:T(2,128)(2,1)}), bf16[16,2,2048]{2,1,0:T(2,128)(2,1)S(1)}, u32[]{:S(2)}, u32[]{:S(2)}) async-start(bf16[16,2,2048]{2,1,0:T(2,128)(2,1)} %reshape.196), calls=%async_computation.4 | async-start | bytes 262144 | tf_op jit(solution)/shard_map/all_to_all | solution.py:148
  73.6 7.4 %all-to-all-done.4 = bf16[16,2,2048]{2,1,0:T(2,128)(2,1)S(1)} async-done(((bf16[16,2,2048]{2,1,0:T(2,128)(2,1)}), bf16[16,2,2048]{2,1,0:T(2,128)(2,1)S(1)}, u32[]{:S(2)}, u32[]{:S(2)}) %all-to-all-start.4) | async-done | bytes 131104 | tf_op jit(solution)/shard_map/all_to_all | solution.py:148
  82.5 11.6 %all_to_all.103 = f32[16,24,128]{2,1,0:T(8,128)S(1)} all-to-all(f32[16,24,128]{2,1,0:T(8,128)S(1)} %copy.71), channel_id=1, replica_groups=mesh['rep'=2,'gx'=16] {'gx'}, dimensions={0} | all-to-all | bytes 393216 | tf_op jit(solution)/shard_map/all_to_all | solution.py:165
  96.3 3.5 %all-to-all-start.6 = ((f32[16,24,128]{2,1,0:T(8,128)}), f32[16,24,128]{2,1,0:T(8,128)S(1)}, u32[]{:S(2)}, u32[]{:S(2)}) async-start(f32[16,24,128]{2,1,0:T(8,128)} %copy.75), calls=%async_computation.6 | async-start | bytes 393216 | tf_op jit(solution)/shard_map/all_to_all | solution.py:176
  99.8 1.0 fusion.47
  100.8 7.9 %all-to-all-done.6 = f32[16,24,128]{2,1,0:T(8,128)S(1)} async-done(((f32[16,24,128]{2,1,0:T(8,128)}), f32[16,24,128]{2,1,0:T(8,128)S(1)}, u32[]{:S(2)}, u32[]{:S(2)}) %all-to-all-start.6) | async-done | bytes 196640 | tf_op jit(solution)/shard_map/all_to_all | solution.py:176
  112.1 3.5 %all-to-all-start.7 = ((bf16[16,2,2048]{2,1,0:T(2,128)(2,1)}), bf16[16,2,2048]{2,1,0:T(2,128)(2,1)S(1)}, u32[]{:S(2)}, u32[]{:S(2)}) async-start(bf16[16,2,2048]{2,1,0:T(2,128)(2,1)} %reshape.198), calls=%async_computation.7 | async-start | bytes 262144 | tf_op jit(solution)/shard_map/all_to_all | solution.py:186
  115.6 1.9 %convolution_add_fusion = f32[16,64,128]{2,1,0:T(8,128)} fusion(f32[16,64,128]{2,1,0:T(8,128)S(1)} %fusion.47, f32[16,16,64]{2,1,0:T(8,128)S(1)} %get-tuple-element.27, f32[16,16,64]{2,0,1:T(8,128)S(1)} %copy_negate_fusion, f32[16,16,64]{2,0,1:T(8,128)S(1)} %copy.95), kind=kOutput, calls=%fused_computation.25 | convolution fusion | flops 25329664 | bytes 1245184 | tf_op jit(solution)/shard_map/ymc,ymf->mcf/dot_general | solution.py:94
  118.9 4.6 %all-to-all-done.7 = bf16[16,2,2048]{2,1,0:T(2,128)(2,1)S(1)} async-done(((bf16[16,2,2048]{2,1,0:T(2,128)(2,1)}), bf16[16,2,2048]{2,1,0:T(2,128)(2,1)S(1)}, u32[]{:S(2)}, u32[]{:S(2)}) %all-to-all-start.7) | async-done | bytes 131104 | tf_op jit(solution)/shard_map/all_to_all | solution.py:186
  124.1 1.1 fusion.13
  (90 shorter events, 19.9 us)
Async XLA Ops:
  0.6 1.1 copy-start
  0.7 0.6 copy-start.3
  2.3 29.9 %copy-start.1 = (bf16[16,64,128]{2,1,0:T(8,128)(2,1)S(1)}, bf16[16,64,128]{2,1,0:T(8,128)(2,1)}, u32[]{:S(2)}) copy-start(bf16[16,64,128]{2,1,0:T(8,128)(2,1)} %param.7) | copy-start | bytes 786436
  3.2 15.3 %all-to-all-start = ((bf16[16,2,2048]{2,1,0:T(2,128)(2,1)}), bf16[16,2,2048]{2,1,0:T(2,128)(2,1)S(1)}, u32[]{:S(2)}, u32[]{:S(2)}) async-start(bf16[16,2,2048]{2,1,0:T(2,128)(2,1)} %reshape.192), calls=%async_computation | async-start | bytes 262144 | tf_op jit(solution)/shard_map/all_to_all | solution.py:136
  19.9 17.5 %copy-start.7 = (bf16[64,128]{1,0:T(8,128)(2,1)S(1)}, bf16[64,128]{1,0:T(8,128)(2,1)}, u32[]{:S(2)}) copy-start(bf16[64,128]{1,0:T(8,128)(2,1)} %param.8) | copy-start | bytes 49156
  20.7 11.4 %all-to-all-start.1 = ((f32[1,256,128]{2,0,1:T(1,128)}), f32[1,256,128]{2,0,1:T(1,128)S(1)}, u32[]{:S(2)}, u32[]{:S(2)}) async-start(f32[1,256,128]{2,0,1:T(1,128)} %bitcast.17), calls=%async_computation.1 | async-start | bytes 262144 | tf_op jit(solution)/shard_map/all_to_all | solution.py:138
  33.8 11.4 %all-to-all-start.2 = ((f32[16,16,128]{2,1,0:T(8,128)}), f32[16,16,128]{2,1,0:T(8,128)S(1)}, u32[]{:S(2)}, u32[]{:S(2)}) async-start(f32[16,16,128]{2,1,0:T(8,128)} %copy.61), calls=%async_computation.2 | async-start | bytes 262144 | tf_op jit(solution)/shard_map/all_to_all | solution.py:140
  37.8 26.0 %copy-start.2 = (f32[128,2,16,128]{3,0,2,1:T(8,128)}, f32[128,2,16,128]{3,0,2,1:T(8,128)S(1)}, u32[]{:S(2)}) copy-start(f32[128,2,16,128]{3,0,2,1:T(8,128)S(1)} %fusion.62) | copy-start | bytes 6291460
  48.5 11.4 %all-to-all-start.3 = ((bf16[16,2,2048]{2,1,0:T(2,128)(2,1)}), bf16[16,2,2048]{2,1,0:T(2,128)(2,1)S(1)}, u32[]{:S(2)}, u32[]{:S(2)}) async-start(bf16[16,2,2048]{2,1,0:T(2,128)(2,1)} %reshape.194), calls=%async_computation.3 | async-start | bytes 262144 | tf_op jit(solution)/shard_map/all_to_all | solution.py:144
  63.8 0.8 copy-start.9
  64.6 3.3 %copy-start.5 = (f32[16,128]{1,0:T(8,128)S(1)}, f32[16,128]{1,0:T(8,128)}, u32[]{:S(2)}) copy-start(f32[16,128]{1,0:T(8,128)} %get-tuple-element.30) | copy-start | bytes 24580
  64.6 3.3 %copy-start.6 = (f32[16,128]{1,0:T(8,128)S(1)}, f32[16,128]{1,0:T(8,128)}, u32[]{:S(2)}) copy-start(f32[16,128]{1,0:T(8,128)} %get-tuple-element.31) | copy-start | bytes 24580
  69.5 11.4 %all-to-all-start.4 = ((bf16[16,2,2048]{2,1,0:T(2,128)(2,1)}), bf16[16,2,2048]{2,1,0:T(2,128)(2,1)S(1)}, u32[]{:S(2)}, u32[]{:S(2)}) async-start(bf16[16,2,2048]{2,1,0:T(2,128)(2,1)} %reshape.196), calls=%async_computation.4 | async-start | bytes 262144 | tf_op jit(solution)/shard_map/all_to_all | solution.py:148
  96.3 12.5 %all-to-all-start.6 = ((f32[16,24,128]{2,1,0:T(8,128)}), f32[16,24,128]{2,1,0:T(8,128)S(1)}, u32[]{:S(2)}, u32[]{:S(2)}) async-start(f32[16,24,128]{2,1,0:T(8,128)} %copy.75), calls=%async_computation.6 | async-start | bytes 393216 | tf_op jit(solution)/shard_map/all_to_all | solution.py:176
  110.4 13.3 %copy-start.4 = (f32[16,128]{1,0:T(8,128)S(1)}, f32[16,128]{1,0:T(8,128)}, u32[]{:S(2)}) copy-start(f32[16,128]{1,0:T(8,128)} %copy-done.3) | copy-start | bytes 24580
  111.2 12.9 %copy-start.8 = (bf16[64,128]{1,0:T(8,128)(2,1)S(1)}, bf16[64,128]{1,0:T(8,128)(2,1)}, u32[]{:S(2)}) copy-start(bf16[64,128]{1,0:T(8,128)(2,1)} %param.8) | copy-start | bytes 49156
  112.1 11.4 %all-to-all-start.7 = ((bf16[16,2,2048]{2,1,0:T(2,128)(2,1)}), bf16[16,2,2048]{2,1,0:T(2,128)(2,1)S(1)}, u32[]{:S(2)}, u32[]{:S(2)}) async-start(bf16[16,2,2048]{2,1,0:T(2,128)(2,1)} %reshape.198), calls=%async_computation.7 | async-start | bytes 262144 | tf_op jit(solution)/shard_map/all_to_all | solution.py:186

commit v2 on v0

v2 whole, which is shorter than its diff:
```python
import functools
import math

import jax
import jax.numpy as jnp
import ml_dtypes
import numpy as np
from jax import lax
from jax.experimental import pallas as pl
from jax.experimental.pallas import tpu as pltpu
from jax.sharding import PartitionSpec as P

KZ = 16
KX = 16
GROUP = 8
LANES = 128
F32 = jnp.float32
BF16 = jnp.bfloat16
PHASES = 10


def make_tables(length_x, length_z):
    z_pos = np.arange(length_z)
    k_z = np.arange(KZ)
    angle_z = 2.0 * math.pi * (k_z[:, None] * z_pos[None, :] % length_z) / length_z
    cos_z, sin_z = np.cos(angle_z), np.sin(angle_z)
    k_weight = np.where(k_z == 0, 1.0, 2.0)[:, None]
    forward_z = np.concatenate([cos_z, -sin_z], 0) / math.sqrt(length_z)
    inverse_z = np.concatenate([k_weight * cos_z, -k_weight * sin_z], 0) / math.sqrt(length_z)
    j_index = np.arange(KX)
    k_x = np.where(j_index < KX // 2, j_index, length_x - KX + j_index)
    x_pos = np.arange(length_x)
    angle_x = 2.0 * math.pi * (k_x[:, None] * x_pos[None, :] % length_x) / length_x
    cosine_x = np.cos(angle_x) / math.sqrt(length_x)
    sine_x = np.sin(angle_x) / math.sqrt(length_x)
    eye = np.eye(KZ)
    kron_c, kron_s = np.kron(cosine_x, eye), np.kron(sine_x, eye)
    forward_x = np.concatenate([kron_c, kron_s], 0)
    inverse_x = np.concatenate([kron_c.T, kron_s.T], 0)

    def low(table):
        return table.astype(np.float32).astype(ml_dtypes.bfloat16)

    return low(forward_z), low(inverse_z), low(forward_x), low(inverse_x)


def gelu_parts(x):
    k = math.sqrt(2.0 / math.pi)
    sq = x * x
    t = jnp.tanh(k * x * (1.0 + 0.044715 * sq))
    half = 0.5 * (1.0 + t)
    slope = half + 0.5 * x * (1.0 - t * t) * (k * (1.0 + 3 * 0.044715 * sq))
    return x * half, slope


def dot(a, b, dims=((1,), (0,))):
    return lax.dot_general(a, b, (dims, ((), ())), preferred_element_type=F32)


NT = ((1,), (1,))
TN = ((0,), (0,))


def loop(low, high, step):
    if high - low <= 4:
        for i in range(low, high):
            step(i)
    else:
        lax.fori_loop(low, high, lambda i, c: (step(i), c)[1], 0)


def kernel(
    n, planes, rows, own, scale,
    field, cot, weight, w_in, w_out, fz, gz, tx, ti,
    out_field, out_spec, out_win, out_wout,
    s1, r1, s4, r4, s5, r5, s8, r8,
    s2, r2, s3, r3, s6, r6, s7, r7,
    sw, rw, sg, rg,
    wfull, xs, ys, ds, act, slope, branch, dw,
    send_sem, recv_sem,
):
    me = lax.axis_index("gx")
    low_lane = lax.broadcasted_iota(jnp.int32, (KZ, LANES), 1) < LANES // 2
    chans = LANES // 2
    per_x = rows // GROUP
    groups = planes * per_x

    barrier = pltpu.get_barrier_semaphore()

    def greet(i, c):
        pl.semaphore_signal(barrier, inc=1, device_id={"gx": lax.rem(me + i, n)})
        return c

    lax.fori_loop(1, n, greet, 0)

    def send(phase, src, dst):
        def one(i, c):
            to = lax.rem(me + i, n)
            pltpu.make_async_remote_copy(
                src_ref=src(to), dst_ref=dst.at[me],
                send_sem=send_sem.at[phase], recv_sem=recv_sem.at[phase],
                device_id={"gx": to},
            ).start()
            return c

        lax.fori_loop(1, n, one, 0)

    def exchange(phase, src, dst):
        send(phase, lambda to: src.at[to], dst)
        dst[me] = src[me]

    def bulk(phase, dst):
        some = dst.at[pl.ds(0, n - 1)]
        return pltpu.make_async_remote_copy(
            src_ref=some, dst_ref=some,
            send_sem=send_sem.at[phase], recv_sem=recv_sem.at[phase],
            device_id={"gx": lax.rem(me + 1, n)},
        )

    def swap(v):
        return pltpu.roll(v, LANES // 2, 1)

    def rotated(v, first):
        lane = lax.broadcasted_iota(jnp.int32, v.shape, 1) < LANES // 2
        turned = swap(v)
        return jnp.where(lane, first * turned, -first * turned)

    def place(g):
        return g // per_x, lax.rem(g, per_x) * GROUP if not isinstance(g, int) else (g % per_x) * GROUP

    def z_forward(g, slabs, table, dst):
        res = dot(table[...], slabs, NT)
        x, y0 = place(g)
        for b in range(GROUP // 2):
            real = res[:KZ, b * LANES:(b + 1) * LANES]
            imag = res[KZ:, b * LANES:(b + 1) * LANES]
            dst[y0 + 2 * b, x] = jnp.where(low_lane, real, swap(imag)).astype(BF16)
            dst[y0 + 2 * b + 1, x] = jnp.where(low_lane, swap(real), imag).astype(BF16)

    def z_inverse(g, src, table):
        x, y0 = place(g)
        pieces = []
        for b in range(GROUP // 2):
            even = src[y0 + 2 * b, x].astype(F32)
            odd = src[y0 + 2 * b + 1, x].astype(F32)
            pieces.append(jnp.concatenate(
                [jnp.where(low_lane, even, swap(odd)), jnp.where(low_lane, swap(even), odd)], 0))
        return dot(jnp.concatenate(pieces, 1).astype(BF16), table[...], TN)

    def x_forward(src, dst):
        data = src[...].reshape(n * planes * KZ, LANES)
        both = dot(tx[...], data)
        half = KX * KZ
        spec = both[:half] + rotated(both[half:], 1.0)
        for d in range(n):
            dst[d] = spec[d * own:(d + 1) * own].astype(dst.dtype)

    def x_inverse(src, dst):
        data = jnp.concatenate([src[d].astype(F32) for d in range(n)], 0).astype(BF16)
        both = dot(ti[...], data)
        half = n * planes * KZ
        res = both[:half] + rotated(both[half:], -1.0)
        dst[...] = res.astype(BF16).reshape(dst.shape)

    def spread(src, dst):
        for d in range(n):
            dst[d * own:(d + 1) * own, :] = src[d].astype(F32)

    def collect(src, dst):
        for d in range(n):
            dst[d] = src[d * own:(d + 1) * own, :].astype(dst.dtype)

    def to_lane(v):
        return jnp.concatenate([v[i * chans:(i + 1) * chans] for i in range(GROUP)], 1)

    def to_row(v):
        return jnp.concatenate([v[:, i * LANES:(i + 1) * LANES] for i in range(GROUP)], 0)

    def slab_rows(ref, g):
        return ref[pl.ds(g * GROUP, GROUP)].reshape(GROUP * chans, LANES)

    def network(g):
        u = to_lane(slab_rows(field, g))
        value, grad = gelu_parts(dot(w_in[...], u, TN))
        value = value.astype(BF16)
        act[g] = value
        slope[g] = grad.astype(BF16)
        branch[g] = to_row(dot(w_out[...], value, TN))

    def network_part(i):
        loop(i * groups // 4, (i + 1) * groups // 4, network)

    loop(0, groups, lambda g: z_forward(g, slab_rows(field, g), fz, s1))
    pl.semaphore_wait(barrier, n - 1)
    exchange(0, s1, r1)
    for m in range(own):
        w = weight[m].astype(F32)
        wfull[m] = jnp.concatenate([w, rotated(w, -1.0)], 0).astype(BF16)
    network_part(0)
    bulk(0, r1).wait_recv()
    x_forward(r1, s2)
    exchange(1, s2, r2)
    network_part(1)
    bulk(1, r2).wait_recv()
    spread(r2, xs)
    for m in range(own):
        at = pl.ds(m, n, stride=own)
        ys[at, :] = dot(xs[at, :].astype(BF16), wfull[m])
    collect(ys, s3)
    exchange(2, s3, r3)
    network_part(2)
    bulk(2, r3).wait_recv()
    x_inverse(r3, s4)
    exchange(3, s4, r4)
    network_part(3)
    bulk(3, r4).wait_recv()

    def point(g):
        pre = z_inverse(g, r4, gz) + branch[g]
        unused, grad = gelu_parts(pre)
        d_pre = (slab_rows(cot, g).astype(F32) * grad).astype(BF16)
        out_field[pl.ds(g * GROUP, GROUP)] = d_pre.reshape(GROUP, chans, LANES)
        z_forward(g, d_pre, gz, s5)

    loop(0, groups, point)
    exchange(4, s5, r5)
    dw[...] = jnp.zeros_like(dw)

    def network_back(g):
        d_pre = to_lane(slab_rows(out_field, g))
        d_act = (slope[g].astype(F32) * dot(w_out[...], d_pre)).astype(BF16)
        branch[g] = to_row(dot(w_in[...], d_act))
        u = to_lane(slab_rows(field, g))
        dw[:chans, :] += dot(u, d_act, NT)
        dw[chans:, :] += dot(d_pre, act[g], NT)

    loop(0, groups // 2, network_back)
    bulk(4, r5).wait_recv()
    x_forward(r5, s6)
    exchange(5, s6, r6)
    loop(groups // 2, groups, network_back)
    share = LANES // n
    for d in range(n):
        sw[d] = dw[d * share:(d + 1) * share, :]
    exchange(8, sw, rw)
    bulk(5, r6).wait_recv()
    spread(r6, ds)
    for m in range(own):
        at = pl.ds(m, n, stride=own)
        ys[at, :] = dot(ds[at, :].astype(BF16), wfull[m], NT)
    collect(ys, s7)
    exchange(6, s7, r7)
    for m in range(own):
        at = pl.ds(m, n, stride=own)
        full = dot(xs[at, :].astype(BF16), ds[at, :].astype(BF16), TN)
        out_spec[m] = full[:chans] + rotated(full[chans:], 1.0)
    bulk(8, rw).wait_recv()
    sg[0] = jnp.sum(rw[...], 0) * scale
    send(9, lambda to: sg.at[0], rg)
    rg[me] = sg[0]
    bulk(6, r7).wait_recv()
    x_inverse(r7, s8)
    exchange(7, s8, r8)
    bulk(9, rg).wait_recv()
    for d in range(n):
        dw[d * share:(d + 1) * share, :] = rg[d]
    out_win[...] = dw[:chans, :]
    out_wout[...] = dw[chans:, :].T
    bulk(7, r8).wait_recv()

    def finish(g):
        du = z_inverse(g, r8, fz) + branch[g]
        out_field[pl.ds(g * GROUP, GROUP)] = du.astype(BF16).reshape(GROUP, chans, LANES)

    loop(0, groups, finish)
    for phase, dst in enumerate((r1, r2, r3, r4, r5, r6, r7, r8, rw, rg)):
        bulk(phase, dst).wait_send()


def body(in_field, cotangent, spec_weight, w_in, w_out):
    n = lax.axis_size("gx")
    planes, rows, chans, z_cells = in_field.shape
    own = spec_weight.shape[0]
    length_x = planes * n
    assert rows == n and z_cells == LANES and 2 * chans == LANES
    fz, gz, tx, ti = make_tables(length_x, z_cells)
    slabs = planes * rows
    groups = slabs // GROUP
    hidden = w_in.shape[1]
    wire = BF16 if own % 16 == 0 else F32
    big = pltpu.VMEM((n, planes, KZ, LANES), BF16)
    small = pltpu.VMEM((n, own, LANES), wire)
    share = LANES // n
    scratch = [big] * 8 + [small] * 8 + [
        pltpu.VMEM((n, share, LANES), F32),
        pltpu.VMEM((n, share, LANES), F32),
        pltpu.VMEM((1, share, LANES), F32),
        pltpu.VMEM((n, share, LANES), F32),
        pltpu.VMEM((own, LANES, LANES), BF16),
        pltpu.VMEM((n * own, LANES), F32),
        pltpu.VMEM((n * own, LANES), F32),
        pltpu.VMEM((n * own, LANES), F32),
        pltpu.VMEM((groups, hidden, GROUP * LANES), BF16),
        pltpu.VMEM((groups, hidden, GROUP * LANES), BF16),
        pltpu.VMEM((groups, GROUP * chans, LANES), F32),
        pltpu.VMEM((LANES, LANES), F32),
        pltpu.SemaphoreType.DMA((PHASES,)),
        pltpu.SemaphoreType.DMA((PHASES,)),
    ]
    scale = 1.0 / math.sqrt(length_x * rows * z_cells)
    vmem = pl.BlockSpec(memory_space=pltpu.VMEM)
    grad_field, grad_spec, grad_w_in, grad_w_out = pl.pallas_call(
        functools.partial(kernel, n, planes, rows, own, scale),
        out_shape=(
            jax.ShapeDtypeStruct((slabs, chans, z_cells), BF16),
            jax.ShapeDtypeStruct(spec_weight.shape, F32),
            jax.ShapeDtypeStruct(w_in.shape, F32),
            jax.ShapeDtypeStruct(w_out.shape, F32),
        ),
        in_specs=[vmem] * 9,
        out_specs=(vmem,) * 4,
        scratch_shapes=scratch,
        compiler_params=pltpu.CompilerParams(
            collective_id=0, has_side_effects=True, vmem_limit_bytes=60 * 1024 * 1024
        ),
    )(
        in_field.reshape(slabs, chans, z_cells),
        cotangent.reshape(slabs, chans, z_cells),
        spec_weight, w_in, w_out,
        jnp.asarray(fz), jnp.asarray(gz), jnp.asarray(tx), jnp.asarray(ti),
    )
    return grad_field.reshape(in_field.shape), grad_spec, grad_w_in, grad_w_out


def solution(mesh):
    placed = (
        P(("rep", "gx"), None, None, None),
        P(("rep", "gx"), None, None, None),
        P("gx", None, None),
        P(),
        P(),
    )
    return jax.shard_map(
        body,
        mesh=mesh,
        in_specs=placed,
        out_specs=(
            P(("rep", "gx"), None, None, None),
            P(("rep", "gx"), None, None),
            P("rep", None),
            P("rep", None),
        ),
        check_vma=False,
    )
```

time: 210 us -> 57.1 us (0.27)
  waiting for transfers between devices: 123 us -> 0 us
  Pallas kernels: 0 us -> 49.8 us
  starting transfers between devices: 35.1 us -> 0 us
  matrix products: 24.9 us -> 0 us
  between operations: 14.5 us -> 0.64 us
  other arithmetic: 2.9 us -> 0 us
  local copies, waits for them, and re-layouts: 8.78 us -> 6.31 us
    psum x1 -> x0, waiting for transfers between devices: 77.6 us -> none  [body(): dw_in, dw_out = lax.psum((dw_in, dw_out), 'gx')]
    pallas_call x0 -> x1, Pallas kernels: none -> 49.8 us  [body(): pl.pallas_call(functools.partial(kernel, n, planes, rows, own, scale), ou...]
    all_to_all x8 -> x0, waiting for transfers between devices: 45.7 us -> none  [the longest x1 7.92 us: body(): lax.all_to_all(coeffs, 'gx', split_axis=1, concat_axis=0, tiled=True)]
    all_to_all x8 -> x0, starting transfers between devices: 35 us -> none  [the longest x1 7.39 us: body(): lax.all_to_all(coeffs, 'gx', split_axis=1, concat_axis=0, tiled=True)]
    dot_general x32 -> x0, matrix products: 24.9 us -> none  [the longest x1 3.29 us: pointwise(): jnp.einsum('xyhz,hc->xycz', act_b, w_out, preferred_element_type=f32)]
    concatenate x6 -> x0, local copies, waits for them, and re-layouts: 3 us -> none  [the longest x2 1.39 us: join_halves(): joined = jnp.concatenate([halves[0], halves[1]], -1)]
    unnamed x28 -> x9, local copies, waits for them, and re-layouts: 5.44 us -> 6.31 us
  transfers between devices with their start and end apart: 9 -> 0, of which waited for: 8 -> 0; matrix products, arithmetic and copies ran while one was open for 6% -> 0% of each run, Pallas kernels for 0% -> 0%
where the time goes in v2:
time: 57.1 us; the launch traced here: 56.8 us
  Pallas kernels  49.8 us (87%)
  local copies, waits for them, and re-layouts  6.31 us (11%)
  between operations  0.64 us (1%)
    pallas_call x1, Pallas kernels, body(): pl.pallas_call(functools.partial(kernel, n, planes, rows, own, scale), ou...  49.8 us
    unnamed x9, local copies, waits for them, and re-layouts  6.31 us

profile of v2, /device:TPU:0, one launch (start us, length us, event | category | flops | bytes accessed | tf_op | source)
XLA Modules:
  0.0 56.8 jit_solution(4686628273343132678)
XLA Ops:
  0.6 1.4 %copy.13.w_out = bf16[128,64]{1,0:T(8,128)(2,1)} copy(bf16[128,64]{0,1:T(8,128)(2,1)} %param.13) | data formatting | bytes 32768 | tf_op args[4]
  2.1 49.8 %shard_map.120 = (bf16[32,64,128]{2,1,0:T(8,128)(2,1)}, f32[16,64,128]{2,1,0:T(8,128)}, f32[64,128]{1,0:T(8,128)}, f32[128,64]{1,0:T(8,128)}) custom-call(bf16[32,64,128]{2,1,0:T(8,128)(2,1)} %bitcast.3, bf16[32,64,128]{2,1,0:T(8,128)(2,1)} %bitcast.4, bf16[16,64,128]{2,1,0:T(8,128)(2,1)} %weight.1, bf16[64,128]{1,0:T(8,128)(2,1)} %w_in.1, ...), custom_call_target="tpu_custom_call" | custom-call | tf_op jit(solution)/shard_map/pallas_call | solution.py:312
  51.9 1.5 %copy.14 = f32[128,64]{0,1:T(8,128)} copy(f32[128,64]{1,0:T(8,128)} %get-tuple-element.15) | data formatting | bytes 65536
  53.4 0.0 copy-start
  53.4 1.9 %copy.18 = bf16[2,16,64,128]{3,2,1,0:T(8,128)(2,1)} copy(bf16[2,16,64,128]{3,2,1,0:T(8,128)(2,1)} %bitcast.5) | data formatting | bytes 1048576
  55.4 0.0 copy-done
  55.4 0.0 copy-start.1
  55.4 0.8 %copy.19 = f32[16,64,128]{2,1,0:T(8,128)} copy(f32[16,64,128]{2,1,0:T(8,128)S(1)} %copy-done) | data formatting | bytes 1048576
  56.2 0.0 copy-done.1
  56.2 0.6 %copy.20 = f32[64,128]{1,0:T(8,128)} copy(f32[64,128]{1,0:T(8,128)S(1)} %copy-done.1) | data formatting | bytes 65536
Async XLA Ops:
  53.4 1.9 %copy-start = (f32[16,64,128]{2,1,0:T(8,128)S(1)}, f32[16,64,128]{2,1,0:T(8,128)}, u32[]{:S(2)}) copy-start(f32[16,64,128]{2,1,0:T(8,128)} %get-tuple-element.21) | copy-start | bytes 1572868
  55.4 0.8 %copy-start.1 = (f32[64,128]{1,0:T(8,128)S(1)}, f32[64,128]{1,0:T(8,128)}, u32[]{:S(2)}) copy-start(f32[64,128]{1,0:T(8,128)} %get-tuple-element.22) | copy-start | bytes 98308

commit v3 on v2

--- a/solution.py
+++ b/solution.py
@@ -61,6 +61,18 @@
 TN = ((0,), (0,))
 
 
+def slabs_of(src, table, x, y0):
+    low_lane = lax.broadcasted_iota(jnp.int32, (KZ, LANES), 1) < LANES // 2
+    pieces = []
+    for b in range(GROUP // 2):
+        even = src[y0 + 2 * b, x].astype(F32)
+        odd = src[y0 + 2 * b + 1, x].astype(F32)
+        real = jnp.where(low_lane, even, pltpu.roll(odd, LANES // 2, 1))
+        imag = jnp.where(low_lane, pltpu.roll(even, LANES // 2, 1), odd)
+        pieces.append(jnp.concatenate([real, imag], 0))
+    return dot(jnp.concatenate(pieces, 1).astype(BF16), table[...], TN)
+
+
 def loop(low, high, step):
     if high - low <= 4:
         for i in range(low, high):
@@ -71,15 +83,23 @@
 
 def kernel(
     n, planes, rows, own, scale,
-    field, cot, weight, w_in, w_out, fz, gz, tx, ti,
-    out_field, out_spec, out_win, out_wout,
+    field_hbm, cot_hbm, weight_hbm, tx_hbm, ti_hbm, w_in, w_out_t, fz, gz,
+    out_field, out_spec, out_dw, out_coeffs,
     s1, r1, s4, r4, s5, r5, s8, r8,
     s2, r2, s3, r3, s6, r6, s7, r7,
     sw, rw, sg, rg,
     wfull, xs, ys, ds, act, slope, branch, dw,
-    send_sem, recv_sem,
+    field, cot, weight, tx, ti,
+    send_sem, recv_sem, load_sem,
 ):
     me = lax.axis_index("gx")
+    loads = [
+        pltpu.make_async_copy(src, dst, load_sem.at[i])
+        for i, (src, dst) in enumerate((
+            (field_hbm, field), (weight_hbm, weight), (tx_hbm, tx), (ti_hbm, ti), (cot_hbm, cot)))
+    ]
+    for load in loads:
+        load.start()
     low_lane = lax.broadcasted_iota(jnp.int32, (KZ, LANES), 1) < LANES // 2
     chans = LANES // 2
     per_x = rows // GROUP
@@ -138,14 +158,7 @@
             dst[y0 + 2 * b + 1, x] = jnp.where(low_lane, swap(real), imag).astype(BF16)
 
     def z_inverse(g, src, table):
-        x, y0 = place(g)
-        pieces = []
-        for b in range(GROUP // 2):
-            even = src[y0 + 2 * b, x].astype(F32)
-            odd = src[y0 + 2 * b + 1, x].astype(F32)
-            pieces.append(jnp.concatenate(
-                [jnp.where(low_lane, even, swap(odd)), jnp.where(low_lane, swap(even), odd)], 0))
-        return dot(jnp.concatenate(pieces, 1).astype(BF16), table[...], TN)
+        return slabs_of(src, table, *place(g))
 
     def x_forward(src, dst):
         data = src[...].reshape(n * planes * KZ, LANES)
@@ -185,18 +198,22 @@
         value = value.astype(BF16)
         act[g] = value
         slope[g] = grad.astype(BF16)
-        branch[g] = to_row(dot(w_out[...], value, TN))
+        branch[g] = to_row(dot(w_out_t[...], value))
 
     def network_part(i):
         loop(i * groups // 4, (i + 1) * groups // 4, network)
 
+    loads[0].wait()
     loop(0, groups, lambda g: z_forward(g, slab_rows(field, g), fz, s1))
     pl.semaphore_wait(barrier, n - 1)
     exchange(0, s1, r1)
+    loads[1].wait()
     for m in range(own):
         w = weight[m].astype(F32)
         wfull[m] = jnp.concatenate([w, rotated(w, -1.0)], 0).astype(BF16)
     network_part(0)
+    for load in loads[2:]:
+        load.wait()
     bulk(0, r1).wait_recv()
     x_forward(r1, s2)
     exchange(1, s2, r2)
@@ -228,8 +245,9 @@
 
     def network_back(g):
         d_pre = to_lane(slab_rows(out_field, g))
-        d_act = (slope[g].astype(F32) * dot(w_out[...], d_pre)).astype(BF16)
-        branch[g] = to_row(dot(w_in[...], d_act))
+        d_act = (slope[g].astype(F32) * dot(w_out_t[...], d_pre, TN)).astype(BF16)
+        du = to_row(dot(w_in[...], d_act))
+        out_field[pl.ds(g * GROUP, GROUP)] = du.astype(BF16).reshape(GROUP, chans, LANES)
         u = to_lane(slab_rows(field, g))
         dw[:chans, :] += dot(u, d_act, NT)
         dw[chans:, :] += dot(d_pre, act[g], NT)
@@ -263,18 +281,35 @@
     exchange(7, s8, r8)
     bulk(9, rg).wait_recv()
     for d in range(n):
-        dw[d * share:(d + 1) * share, :] = rg[d]
-    out_win[...] = dw[:chans, :]
-    out_wout[...] = dw[chans:, :].T
+        out_dw[d * share:(d + 1) * share, :] = rg[d]
     bulk(7, r8).wait_recv()
-
-    def finish(g):
-        du = z_inverse(g, r8, fz) + branch[g]
-        out_field[pl.ds(g * GROUP, GROUP)] = du.astype(BF16).reshape(GROUP, chans, LANES)
-
-    loop(0, groups, finish)
+    out_coeffs[...] = r8[...]
     for phase, dst in enumerate((r1, r2, r3, r4, r5, r6, r7, r8, rw, rg)):
         bulk(phase, dst).wait_send()
+
+
+def finish_kernel(
+    planes, rows, coeffs, network, spec, dw, fz, out_field, out_spec, out_win, out_wout_t, sems
+):
+    chans = LANES // 2
+    per_x = rows // GROUP
+    copies = [
+        pltpu.make_async_copy(spec, out_spec, sems.at[0]),
+        pltpu.make_async_copy(dw.at[pl.ds(0, chans)], out_win, sems.at[1]),
+        pltpu.make_async_copy(dw.at[pl.ds(chans, chans)], out_wout_t, sems.at[2]),
+    ]
+    for copy in copies:
+        copy.start()
+
+    def finish(g):
+        x, y0 = g // per_x, (g % per_x if isinstance(g, int) else lax.rem(g, per_x)) * GROUP
+        at = pl.ds(g * GROUP, GROUP)
+        du = slabs_of(coeffs, fz, x, y0) + network[at].reshape(GROUP * chans, LANES).astype(F32)
+        out_field[at] = du.astype(BF16).reshape(GROUP, chans, LANES)
+
+    loop(0, planes * per_x, finish)
+    for copy in copies:
+        copy.wait()
 
 
 def body(in_field, cotangent, spec_weight, w_in, w_out):
@@ -304,20 +339,30 @@
         pltpu.VMEM((groups, hidden, GROUP * LANES), BF16),
         pltpu.VMEM((groups, GROUP * chans, LANES), F32),
         pltpu.VMEM((LANES, LANES), F32),
+        pltpu.VMEM((slabs, chans, z_cells), BF16),
+        pltpu.VMEM((slabs, chans, z_cells), BF16),
+        pltpu.VMEM(spec_weight.shape, BF16),
+        pltpu.VMEM(tx.shape, BF16),
+        pltpu.VMEM(ti.shape, BF16),
         pltpu.SemaphoreType.DMA((PHASES,)),
         pltpu.SemaphoreType.DMA((PHASES,)),
+        pltpu.SemaphoreType.DMA((5,)),
     ]
     scale = 1.0 / math.sqrt(length_x * rows * z_cells)
     vmem = pl.BlockSpec(memory_space=pltpu.VMEM)
-    grad_field, grad_spec, grad_w_in, grad_w_out = pl.pallas_call(
+    hbm = pl.BlockSpec(memory_space=pl.ANY)
+    field_shape = jax.ShapeDtypeStruct((slabs, chans, z_cells), BF16)
+    spec_shape = jax.ShapeDtypeStruct(spec_weight.shape, F32)
+    fz, gz = jnp.asarray(fz), jnp.asarray(gz)
+    network, spec, dw, coeffs = pl.pallas_call(
         functools.partial(kernel, n, planes, rows, own, scale),
         out_shape=(
-            jax.ShapeDtypeStruct((slabs, chans, z_cells), BF16),
-            jax.ShapeDtypeStruct(spec_weight.shape, F32),
-            jax.ShapeDtypeStruct(w_in.shape, F32),
-            jax.ShapeDtypeStruct(w_out.shape, F32),
+            field_shape,
+            spec_shape,
+            jax.ShapeDtypeStruct((LANES, LANES), F32),
+            jax.ShapeDtypeStruct((n, planes, KZ, LANES), BF16),
         ),
-        in_specs=[vmem] * 9,
+        in_specs=[hbm] * 5 + [vmem] * 4,
         out_specs=(vmem,) * 4,
         scratch_shapes=scratch,
         compiler_params=pltpu.CompilerParams(
@@ -326,10 +371,22 @@
     )(
         in_field.reshape(slabs, chans, z_cells),
         cotangent.reshape(slabs, chans, z_cells),
-        spec_weight, w_in, w_out,
-        jnp.asarray(fz), jnp.asarray(gz), jnp.asarray(tx), jnp.asarray(ti),
+        spec_weight, jnp.asarray(tx), jnp.asarray(ti), w_in, w_out.T, fz, gz,
     )
-    return grad_field.reshape(in_field.shape), grad_spec, grad_w_in, grad_w_out
+    grad_field, grad_spec, grad_w_in, grad_w_out_t = pl.pallas_call(
+        functools.partial(finish_kernel, planes, rows),
+        out_shape=(
+            field_shape,
+            spec_shape,
+            jax.ShapeDtypeStruct(w_in.shape, F32),
+            jax.ShapeDtypeStruct(w_out.shape[::-1], F32),
+        ),
+        in_specs=[vmem, vmem, hbm, hbm, vmem],
+        out_specs=(vmem, hbm, hbm, hbm),
+        scratch_shapes=[pltpu.SemaphoreType.DMA((3,))],
+        compiler_params=pltpu.CompilerParams(vmem_limit_bytes=32 * 1024 * 1024),
+    )(coeffs, network, spec, dw, fz)
+    return grad_field.reshape(in_field.shape), grad_spec, grad_w_in, grad_w_out_t.T
 
 
 def solution(mesh):

time: 57.1 us -> 54.7 us (0.958)
  local copies, waits for them, and re-layouts: 6.31 us -> 3.83 us
    unnamed x9 -> x10, local copies, waits for them, and re-layouts: 6.31 us -> 3.83 us
    pallas_call x0 -> x1, Pallas kernels: none -> 1.62 us  [body(): pl.pallas_call(functools.partial(finish_kernel, planes, rows), out_shape=...]
    pallas_call x1, Pallas kernels: 49.8 us -> 48.3 us  [body(): pl.pallas_call(functools.partial(kernel, n, planes, rows, own, scale), ou...]
where the time goes in v3:
time: 54.7 us; the launch traced here: 54.4 us
  Pallas kernels  49.9 us (91%)
  local copies, waits for them, and re-layouts  3.83 us (7%)
  between operations  0.67 us (1%)
    pallas_call x1, Pallas kernels, body(): pl.pallas_call(functools.partial(kernel, n, planes, rows, own, scale), ou...  48.3 us
    unnamed x10, local copies, waits for them, and re-layouts  3.83 us
    pallas_call x1, Pallas kernels, body(): pl.pallas_call(functools.partial(finish_kernel, planes, rows), out_shape=...  1.62 us

profile of v3, /device:TPU:0, one launch (start us, length us, event | category | flops | bytes accessed | tf_op | source)
XLA Modules:
  0.0 54.4 jit_solution(1779522946247795575)
XLA Ops:
  0.6 0.0 copy-start.4
  0.6 48.3 %shard_map.120 = (bf16[32,64,128]{2,1,0:T(8,128)(2,1)}, f32[16,64,128]{2,1,0:T(8,128)}, f32[128,128]{1,0:T(8,128)}, bf16[16,2,16,128]{3,2,1,0:T(8,128)(2,1)}) custom-call(bf16[32,64,128]{2,1,0:T(8,128)(2,1)} %bitcast.5, bf16[32,64,128]{2,1,0:T(8,128)(2,1)} %bitcast.6, bf16[16,64,128]{2,1,0:T(8,128)(2,1)} %weight_hbm.1, ...), custom_call_target="tpu_custom_call" | custom-call | tf_op jit(solution)/shard_map/pallas_call | solution.py:357
  48.9 0.0 copy-done.4
  48.9 0.0 copy-start
  49.0 1.0 %copy-done = bf16[32,64,128]{2,1,0:T(8,128)(2,1)S(1)} copy-done((bf16[32,64,128]{2,1,0:T(8,128)(2,1)S(1)}, bf16[32,64,128]{2,1,0:T(8,128)(2,1)}, u32[]{:S(2)}) %copy-start) | copy-done | bytes 524312
  50.0 0.0 copy-start.1
  50.0 1.0 %copy-done.1 = f32[16,64,128]{2,1,0:T(8,128)S(1)} copy-done((f32[16,64,128]{2,1,0:T(8,128)S(1)}, f32[16,64,128]{2,1,0:T(8,128)}, u32[]{:S(2)}) %copy-start.1) | copy-done | bytes 524312
  51.0 0.0 copy-start.2
  51.0 0.9 %copy-done.2 = bf16[16,2,16,128]{3,2,1,0:T(8,128)(2,1)S(1)} copy-done((bf16[16,2,16,128]{3,2,1,0:T(8,128)(2,1)S(1)}, bf16[16,2,16,128]{3,2,1,0:T(8,128)(2,1)}, u32[]{:S(2)}) %copy-start.2) | copy-done | bytes 131096
  51.9 0.0 copy-start.3
  51.9 0.8 %copy-done.3 = f32[128,128]{1,0:T(8,128)S(1)} copy-done((f32[128,128]{1,0:T(8,128)S(1)}, f32[128,128]{1,0:T(8,128)}, u32[]{:S(2)}) %copy-start.3) | copy-done | bytes 65560
  52.8 1.6 %shard_map.121 = (bf16[32,64,128]{2,1,0:T(8,128)(2,1)}, f32[16,64,128]{2,1,0:T(8,128)}, f32[64,128]{1,0:T(8,128)}, f32[64,128]{1,0:T(8,128)}) custom-call(bf16[16,2,16,128]{3,2,1,0:T(8,128)(2,1)S(1)} %copy-done.2, bf16[32,64,128]{2,1,0:T(8,128)(2,1)S(1)} %copy-done, f32[16,64,128]{2,1,0:T(8,128)S(1)} %copy-done.1, f32[128,128]{1,0:T(8,128)S(1)} %copy-done.3, ...), custom_call_target="tpu_custom_call" | custom-call | tf_op jit(solution)/shard_map/pallas_call | solution.py:376
Async XLA Ops:
  0.6 48.3 %copy-start.4 = (bf16[32,128]{1,0:T(8,128)(2,1)S(1)}, bf16[32,128]{1,0:T(8,128)(2,1)}, u32[]{:S(2)}) copy-start(bf16[32,128]{1,0:T(8,128)(2,1)} %constant.8.clone.fz) | copy-start | bytes 24580
  48.9 1.0 %copy-start = (bf16[32,64,128]{2,1,0:T(8,128)(2,1)S(1)}, bf16[32,64,128]{2,1,0:T(8,128)(2,1)}, u32[]{:S(2)}) copy-start(bf16[32,64,128]{2,1,0:T(8,128)(2,1)} %get-tuple-element.13.network) | copy-start | bytes 1572868
  50.0 1.0 %copy-start.1 = (f32[16,64,128]{2,1,0:T(8,128)S(1)}, f32[16,64,128]{2,1,0:T(8,128)}, u32[]{:S(2)}) copy-start(f32[16,64,128]{2,1,0:T(8,128)} %get-tuple-element.14.spec) | copy-start | bytes 1572868
  51.0 0.9 %copy-start.2 = (bf16[16,2,16,128]{3,2,1,0:T(8,128)(2,1)S(1)}, bf16[16,2,16,128]{3,2,1,0:T(8,128)(2,1)}, u32[]{:S(2)}) copy-start(bf16[16,2,16,128]{3,2,1,0:T(8,128)(2,1)} %get-tuple-element.12.coeffs) | copy-start | bytes 393220
  51.9 0.8 %copy-start.3 = (f32[128,128]{1,0:T(8,128)S(1)}, f32[128,128]{1,0:T(8,128)}, u32[]{:S(2)}) copy-start(f32[128,128]{1,0:T(8,128)} %get-tuple-element.15.dw) | copy-start | bytes 196612

commit v4 on v3

--- a/solution.py
+++ b/solution.py
@@ -384,7 +384,7 @@
         in_specs=[vmem, vmem, hbm, hbm, vmem],
         out_specs=(vmem, hbm, hbm, hbm),
         scratch_shapes=[pltpu.SemaphoreType.DMA((3,))],
-        compiler_params=pltpu.CompilerParams(vmem_limit_bytes=32 * 1024 * 1024),
+        compiler_params=pltpu.CompilerParams(vmem_limit_bytes=63 * 1024 * 1024),
     )(coeffs, network, spec, dw, fz)
     return grad_field.reshape(in_field.shape), grad_spec, grad_w_in, grad_w_out_t.T
 

time: 54.7 us -> 70 us (1.28)
  Pallas kernels: 49.9 us -> 69.1 us
  local copies, waits for them, and re-layouts: 3.83 us -> 0 us
    pallas_call x1, Pallas kernels: 1.62 us -> 20.9 us  [body(): pl.pallas_call(functools.partial(finish_kernel, planes, rows), out_shape=...]
    unnamed x10 -> x0, local copies, waits for them, and re-layouts: 3.83 us -> none
where the time goes in v4:
time: 70 us; the launch traced here: 69.8 us
  Pallas kernels  69.1 us (99%)
    pallas_call x1, Pallas kernels, body(): pl.pallas_call(functools.partial(kernel, n, planes, rows, own, scale), ou...  48.3 us
    pallas_call x1, Pallas kernels, body(): pl.pallas_call(functools.partial(finish_kernel, planes, rows), out_shape=...  20.9 us

profile of v4, /device:TPU:0, one launch (start us, length us, event | category | flops | bytes accessed | tf_op | source)
XLA Modules:
  0.0 69.8 jit_solution(13922737813446322407)
XLA Ops:
  0.6 48.3 %shard_map.120 = (bf16[32,64,128]{2,1,0:T(8,128)(2,1)}, f32[16,64,128]{2,1,0:T(8,128)}, f32[128,128]{1,0:T(8,128)}, bf16[16,2,16,128]{3,2,1,0:T(8,128)(2,1)}) custom-call(bf16[32,64,128]{2,1,0:T(8,128)(2,1)} %bitcast.5, bf16[32,64,128]{2,1,0:T(8,128)(2,1)} %bitcast.6, bf16[16,64,128]{2,1,0:T(8,128)(2,1)} %weight_hbm.1, ...), custom_call_target="tpu_custom_call" | custom-call | tf_op jit(solution)/shard_map/pallas_call | solution.py:357
  48.9 20.9 %shard_map.121 = (bf16[32,64,128]{2,1,0:T(8,128)(2,1)}, f32[16,64,128]{2,1,0:T(8,128)}, f32[64,128]{1,0:T(8,128)}, f32[64,128]{1,0:T(8,128)}) custom-call(bf16[16,2,16,128]{3,2,1,0:T(8,128)(2,1)} %get-tuple-element.12.coeffs, bf16[32,64,128]{2,1,0:T(8,128)(2,1)} %get-tuple-element.13.network, f32[16,64,128]{2,1,0:T(8,128)} %get-tuple-element.14.spec, ...), custom_call_target="tpu_custom_call" | custom-call | tf_op jit(solution)/shard_map/pallas_call | solution.py:376

commit v5 on v4

--- a/solution.py
+++ b/solution.py
@@ -289,17 +289,13 @@
 
 
 def finish_kernel(
-    planes, rows, coeffs, network, spec, dw, fz, out_field, out_spec, out_win, out_wout_t, sems
+    planes, rows, coeffs, network, spec, dw, fz, out_field, out_spec, out_win, out_wout_t
 ):
     chans = LANES // 2
     per_x = rows // GROUP
-    copies = [
-        pltpu.make_async_copy(spec, out_spec, sems.at[0]),
-        pltpu.make_async_copy(dw.at[pl.ds(0, chans)], out_win, sems.at[1]),
-        pltpu.make_async_copy(dw.at[pl.ds(chans, chans)], out_wout_t, sems.at[2]),
-    ]
-    for copy in copies:
-        copy.start()
+    out_spec[...] = spec[...]
+    out_win[...] = dw[:chans, :]
+    out_wout_t[...] = dw[chans:, :]
 
     def finish(g):
         x, y0 = g // per_x, (g % per_x if isinstance(g, int) else lax.rem(g, per_x)) * GROUP
@@ -308,8 +304,6 @@
         out_field[at] = du.astype(BF16).reshape(GROUP, chans, LANES)
 
     loop(0, planes * per_x, finish)
-    for copy in copies:
-        copy.wait()
 
 
 def body(in_field, cotangent, spec_weight, w_in, w_out):
@@ -381,9 +375,8 @@
             jax.ShapeDtypeStruct(w_in.shape, F32),
             jax.ShapeDtypeStruct(w_out.shape[::-1], F32),
         ),
-        in_specs=[vmem, vmem, hbm, hbm, vmem],
-        out_specs=(vmem, hbm, hbm, hbm),
-        scratch_shapes=[pltpu.SemaphoreType.DMA((3,))],
+        in_specs=[vmem] * 5,
+        out_specs=(vmem,) * 4,
         compiler_params=pltpu.CompilerParams(vmem_limit_bytes=63 * 1024 * 1024),
     )(coeffs, network, spec, dw, fz)
     return grad_field.reshape(in_field.shape), grad_spec, grad_w_in, grad_w_out_t.T

time: 70 us -> 51.9 us (0.74)
  Pallas kernels: 69.1 us -> 50.9 us
    pallas_call x1, Pallas kernels: 20.9 us -> 2.67 us  [body(): pl.pallas_call(functools.partial(finish_kernel, planes, rows), out_shape=...]
where the time goes in v5:
time: 51.9 us; the launch traced here: 51.6 us
  Pallas kernels  50.9 us (98%)
  between operations  0.64 us (1%)
    pallas_call x1, Pallas kernels, body(): pl.pallas_call(functools.partial(kernel, n, planes, rows, own, scale), ou...  48.3 us
    pallas_call x1, Pallas kernels, body(): pl.pallas_call(functools.partial(finish_kernel, planes, rows), out_shape=...  2.67 us

profile of v5, /device:TPU:0, one launch (start us, length us, event | category | flops | bytes accessed | tf_op | source)
XLA Modules:
  0.0 51.6 jit_solution(14498335369108248711)
XLA Ops:
  0.6 48.3 %shard_map.120 = (bf16[32,64,128]{2,1,0:T(8,128)(2,1)}, f32[16,64,128]{2,1,0:T(8,128)}, f32[128,128]{1,0:T(8,128)}, bf16[16,2,16,128]{3,2,1,0:T(8,128)(2,1)}) custom-call(bf16[32,64,128]{2,1,0:T(8,128)(2,1)} %bitcast.5, bf16[32,64,128]{2,1,0:T(8,128)(2,1)} %bitcast.6, bf16[16,64,128]{2,1,0:T(8,128)(2,1)} %weight_hbm.1, ...), custom_call_target="tpu_custom_call" | custom-call | tf_op jit(solution)/shard_map/pallas_call | solution.py:351
  48.9 2.7 %shard_map.121 = (bf16[32,64,128]{2,1,0:T(8,128)(2,1)}, f32[16,64,128]{2,1,0:T(8,128)}, f32[64,128]{1,0:T(8,128)}, f32[64,128]{1,0:T(8,128)}) custom-call(bf16[16,2,16,128]{3,2,1,0:T(8,128)(2,1)} %get-tuple-element.12.coeffs, bf16[32,64,128]{2,1,0:T(8,128)(2,1)} %get-tuple-element.13.network, f32[16,64,128]{2,1,0:T(8,128)} %get-tuple-element.14.spec, ...), custom_call_target="tpu_custom_call" | custom-call | tf_op jit(solution)/shard_map/pallas_call | solution.py:370
